TPU v7x, 32 devices: a whole 2x2x4 slice. The times are simulated.
32 devices in a mesh: row: 8 (over z, core), col: 4 (over y, x).
Axes of the slice: x: 2, y: 2, z: 4, core: 2. Of those that a mesh axis runs over, the one named last changes fastest.
Arguments:
- matrix: float32 [16, 8, 128, 32, 4, 128], P(None, 'row', None, None, 'col'), as said below
Outputs:
- swept: float32 [16, 8, 128, 32, 4, 128], P(None, 'row', None, None, 'col')
Inputs may be any that keep to these rules, and one draw needn't show every extreme that they name: `matrix`: every diagonal entry is at least sqrt(16384) - 6 and every off-diagonal entry has magnitude at most 6.
All inputs are finite; a program needn't handle non-finite values.
Results may differ from a plain program's by a relative error of at most 0.0001.
Values sent between devices are 32-bit elements; how exact they have to be, the bound alone decides.
A program may use at most 256 MiB of HBM per device.

v0:
```python
import jax
import jax.numpy as jnp
from jax import lax
from jax.sharding import PartitionSpec as P

PIVOTS = 3


def spread(value, axis, source):
    kept = jnp.where(lax.axis_index(axis) == source, value, 0).astype(value.dtype)
    return lax.psum(kept, axis)


def newton_inverse(block):
    inv_diag = 1.0 / jnp.diagonal(block)
    return 2.0 * jnp.diag(inv_diag) - inv_diag[:, None] * block * inv_diag[None, :]


def send_panel(columns, col_root):
    return spread(columns, "col", col_root)


def scale_rows(inverse, owner_rows, col_slot, col_root, grid_col):
    product = jnp.einsum("ij,jcl->icl", inverse, owner_rows, precision=lax.Precision.HIGHEST)
    kept = jnp.where(grid_col == col_root, inverse, product[:, col_slot])
    return product.at[:, col_slot].set(kept)


def make_rows(matrix_local, col_panel, pivot, grid_row, grid_col, n_row, n_col):
    row_root = pivot % n_row
    row_slot = pivot // n_row
    col_root = pivot % n_col
    col_slot = pivot // n_col
    tile_size = col_panel.shape[1]
    owner = grid_row == row_root
    safe_block = jnp.where(owner, col_panel[row_slot], jnp.eye(tile_size, dtype=jnp.float32))
    inverse = newton_inverse(safe_block)

    def normalize():
        return scale_rows(inverse, matrix_local[row_slot], col_slot, col_root, grid_col)

    def nothing():
        return jnp.zeros(matrix_local[row_slot].shape, jnp.float32)

    rows_out = lax.cond(owner, normalize, nothing)
    return spread(rows_out, "row", row_root)


def update_cols(cols_local, rows_sub, col_panel, pivot, first, grid_row, grid_col, n_row, n_col):
    row_root = pivot % n_row
    row_slot = pivot // n_row
    col_root = pivot % n_col
    col_slot = pivot // n_col
    count = cols_local.shape[2]
    tile_ids = first + jnp.arange(count)
    cleared = (tile_ids == col_slot) & (grid_col == col_root)
    zeroed = jnp.where(cleared[None, None, :, None], jnp.float32(0.0), cols_local)
    result = zeroed - jnp.einsum(
        "aij,jcl->aicl", col_panel, rows_sub, precision=lax.Precision.HIGHEST
    )
    replaced = jnp.where(grid_row == row_root, rows_sub, result[row_slot])
    return result.at[row_slot].set(replaced)


def local(matrix):
    n_row = lax.axis_size("row")
    n_col = lax.axis_size("col")
    grid_row = lax.axis_index("row")
    grid_col = lax.axis_index("col")
    row_tiles, _, tile_size, col_tiles, _, _ = matrix.shape
    matrix_local = matrix.reshape(row_tiles, tile_size, col_tiles, tile_size)
    col_panel = send_panel(matrix_local[:, :, 0, :], 0)
    for pivot in range(PIVOTS):
        pivot_rows = make_rows(matrix_local, col_panel, pivot, grid_row, grid_col, n_row, n_col)
        if pivot + 1 < PIVOTS:
            next_slot = (pivot + 1) // n_col
            next_root = (pivot + 1) % n_col
            middle = update_cols(
                matrix_local[:, :, next_slot : next_slot + 1],
                pivot_rows[:, next_slot : next_slot + 1],
                col_panel,
                pivot,
                next_slot,
                grid_row,
                grid_col,
                n_row,
                n_col,
            )
            next_panel = send_panel(middle[:, :, 0, :], next_root)
            front = update_cols(
                matrix_local[:, :, :next_slot],
                pivot_rows[:, :next_slot],
                col_panel,
                pivot,
                0,
                grid_row,
                grid_col,
                n_row,
                n_col,
            )
            behind = update_cols(
                matrix_local[:, :, next_slot + 1 :],
                pivot_rows[:, next_slot + 1 :],
                col_panel,
                pivot,
                next_slot + 1,
                grid_row,
                grid_col,
                n_row,
                n_col,
            )
            matrix_local = jnp.concatenate([front, middle, behind], axis=2)
            col_panel = next_panel
        else:
            matrix_local = update_cols(
                matrix_local, pivot_rows, col_panel, pivot, 0, grid_row, grid_col, n_row, n_col
            )
    return matrix_local.reshape(matrix.shape)


def solution(mesh):
    in_specs = (P(None, "row", None, None, "col", None),)
    out_specs = P(None, "row", None, None, "col", None)
    return jax.shard_map(local, mesh=mesh, in_specs=in_specs, out_specs=out_specs, check_vma=False)
```

profile of v0, /device:TPU:24, one launch (start us, length us, event | category | flops | bytes accessed | tf_op | source)
XLA Modules:
  0.0 543.3 jit_solution(2617250547564642203)
XLA Ops:
  6.5 0.0 all-reduce.7.cloned.1.call-start
  6.5 31.8 %copy.12 = f32[16,1,128,32,1,128]{5,2,3,0,4,1:T(8,128)} copy(f32[16,1,128,32,1,128]{5,4,3,2,1,0:T(1,128)} %param.23) | data formatting | bytes 67108864 | tf_op args[0]
  38.3 2.3 select_bitcast_fusion.2
  40.6 0.0 all-reduce.7.cloned.1.call-update
  40.7 0.0 all-reduce.9.cloned.1.call-start
  40.8 53.6 %all-reduce.7.cloned.1.call-done = f32[16,128,128]{2,1,0:T(8,128)} async-done(((f32[16,128,128]{2,1,0:T(8,128)}), f32[16,128,128]{2,1,0:T(8,128)}) %all-reduce.7.cloned.1.call-update) | async-done | bytes 1048592 | tf_op jit(solution)/shard_map/psum | solution.py:11
  94.4 1.6 conditional.3
  94.4 1.6 broadcast.250
  96.0 1.5 broadcast_select_fusion.2
  97.5 0.0 copy-start.3
  97.5 0.0 all-reduce.9.cloned.1.call-update
  97.5 0.0 all-reduce.11.cloned.1.call-start
  97.6 69.5 %all-reduce.9.cloned.1.call-done = f32[128,32,128]{2,0,1:T(8,128)} async-done(((f32[128,32,128]{2,0,1:T(8,128)}), f32[128,32,128]{2,0,1:T(8,128)}) %all-reduce.9.cloned.1.call-update) | async-done | bytes 2097168 | tf_op jit(solution)/shard_map/psum | solution.py:11
  167.1 0.0 copy-done.3
  167.1 2.2 fusion.38
  169.3 0.9 fusion.48
  170.2 1.1 select_bitcast_fusion.1
  171.2 0.0 all-reduce.11.cloned.1.call-update
  171.3 0.0 all-reduce.13.cloned.1.call-start
  171.3 0.0 copy-start.2
  171.3 34.3 %fusion.23 = f32[16,128,31,128]{3,1,2,0:T(8,128)} fusion(f32[16,128,32,128]{3,1,2,0:T(8,128)} %bitcast.183, pred[31]{0:T(512)(128)(4,1)S(1)} %compare_and_fusion.2, f32[128,32,128]{2,0,1:T(8,128)} %all-reduce.9.cloned.1.call-done, f32[16,128,128]{2,1,0:T(8,128)S(1)} %copy-done.3), kind=kOutput, calls=%fused_computation.45 | convolution fusion | flops 12498501632 | bytes 68091936 | tf_op jit(solution)/shard_map/aij,jcl->aicl/dot_general | solution.py:58
  205.6 0.0 copy-done.2
  205.7 3.2 fusion.33
  208.8 16.1 %all-reduce.11.cloned.1.call-done = f32[16,128,128]{2,1,0:T(8,128)} async-done(((f32[16,128,128]{2,1,0:T(8,128)}), f32[16,128,128]{2,1,0:T(8,128)}) %all-reduce.11.cloned.1.call-update) | async-done | bytes 1048592 | tf_op jit(solution)/shard_map/psum | solution.py:11
  224.9 1.6 conditional.4
  224.9 1.6 broadcast.252
  226.5 1.5 broadcast_select_fusion.1
  228.0 0.0 copy-start.4
  228.0 0.0 all-reduce.13.cloned.1.call-update
  228.0 0.0 all-reduce.15.cloned.1.call-start
  228.1 69.0 %all-reduce.13.cloned.1.call-done = f32[128,32,128]{2,0,1:T(8,128)} async-done(((f32[128,32,128]{2,0,1:T(8,128)}), f32[128,32,128]{2,0,1:T(8,128)}) %all-reduce.13.cloned.1.call-update) | async-done | bytes 2097168 | tf_op jit(solution)/shard_map/psum | solution.py:11
  297.1 0.0 copy-done.4
  297.1 1.8 fusion.39
  298.9 0.0 copy-start.1
  298.9 1.0 fusion.45
  299.9 1.0 select_bitcast_fusion
  300.9 0.0 all-reduce.15.cloned.1.call-update
  301.0 0.0 all-reduce.17.cloned.1.call-start
  301.0 0.0 copy-done.1
  301.0 34.2 %select_subtract_fusion.1 = f32[16,128,31,128]{3,1,2,0:T(8,128)} fusion(f32[16,128,31,128]{3,1,2,0:T(8,128)} %fusion.33, pred[31]{0:T(512)(128)(4,1)S(1)} %compare_and_fusion.1, f32[128,32,128]{2,0,1:T(8,128)S(1)} %copy-done.1, f32[16,128,128]{2,1,0:T(8,128)} %all-reduce.11.cloned.1.call-done), kind=kOutput, calls=%fused_computation.46 | convolution fusion | flops 12498501632 | bytes 68092416 | tf_op jit(solution)/shard_map/aij,jcl->aicl/dot_general | solution.py:58
  335.2 3.2 fusion.30
  338.4 23.0 %pad_maximum_fusion.1 = f32[16,128,32,128]{3,1,2,0:T(8,128)} fusion(f32[16,128,31,128]{3,1,2,0:T(8,128)} %fusion.30, f32[16,128,1,128]{3,1,2,0:T(8,128)S(1)} %fusion.45), kind=kLoop, calls=%fused_computation.41 | loop fusion | flops 8388608 | bytes 67108864 | tf_op jit(solution)/shard_map/concatenate | solution.py:112
  361.3 0.0 all-reduce.15.cloned.1.call-done
  361.3 1.6 conditional.5
  361.3 1.6 broadcast.254
  362.9 1.5 broadcast_select_fusion
  364.4 0.0 copy-start.5
  364.4 0.0 all-reduce.17.cloned.1.call-update
  364.5 72.3 %all-reduce.17.cloned.1.call-done = f32[128,32,128]{2,0,1:T(8,128)} async-done(((f32[128,32,128]{2,0,1:T(8,128)}), f32[128,32,128]{2,0,1:T(8,128)}) %all-reduce.17.cloned.1.call-update) | async-done | bytes 2097168 | tf_op jit(solution)/shard_map/psum | solution.py:11
  436.8 0.0 copy-done.5
  436.8 34.8 %select_subtract_fusion = f32[16,128,32,128]{3,1,2,0:T(8,128)} fusion(pred[32]{0:T(512)(128)(4,1)S(1)} %compare_and_fusion, f32[128,32,128]{2,0,1:T(8,128)} %all-reduce.17.cloned.1.call-done, f32[16,128,128]{2,1,0:T(8,128)S(1)} %copy-done.5, f32[16,128,31,128]{3,1,2,0:T(8,128)} %fusion.30, f32[16,128,1,128]{3,1,2,0:T(8,128)S(1)} %fusion.45), kind=kOutput, calls=%fused_computation.43 | convolution fusion | flops 12910067712 | bytes 70254624 | tf_op jit(solution)/shard_map/aij,jcl->aicl/dot_general | solution.py:58
  471.6 0.0 copy-start
  471.6 23.1 %copy.32 = f32[16,1,128,32,1,128]{5,2,3,0,4,1:T(8,128)} copy(f32[16,1,128,32,1,128]{5,2,3,0,4,1:T(8,128)} %bitcast.184) | data formatting | bytes 67108864
  494.7 0.0 copy-done
  494.7 3.2 fusion.26
  497.9 38.6 %copy.7 = f32[16,1,128,32,1,128]{5,4,3,2,1,0:T(1,128)} copy(f32[16,1,128,32,1,128]{5,2,3,0,4,1:T(8,128)} %fusion.26) | data formatting | bytes 67108864 | tf_op jit(solution)/shard_map/scatter | solution.py:62
  (8 shorter events, 0.1 us)
Async XLA Ops:
  6.5 87.8 %all-reduce.7.cloned.1.call-start = ((), (), s32[]{:S(2)}) async-start(), calls=%async_computation | async-start | bytes 2097152 | tf_op jit(solution)/shard_map/psum | solution.py:11
  40.7 126.4 %all-reduce.9.cloned.1.call-start = ((), (), s32[]{:S(2)}) async-start(), calls=%async_computation.1 | async-start | bytes 4194304 | tf_op jit(solution)/shard_map/psum | solution.py:11
  97.5 69.6 %copy-start.3 = (f32[16,128,128]{2,1,0:T(8,128)S(1)}, f32[16,128,128]{2,1,0:T(8,128)}, u32[]{:S(2)}) copy-start(f32[16,128,128]{2,1,0:T(8,128)} %all-reduce.7.cloned.1.call-done) | copy-start | bytes 3145732
  97.5 127.4 %all-reduce.11.cloned.1.call-start = ((), (), s32[]{:S(2)}) async-start(), calls=%async_computation.2 | async-start | bytes 2097152 | tf_op jit(solution)/shard_map/psum | solution.py:11
  171.3 125.8 %all-reduce.13.cloned.1.call-start = ((), (), s32[]{:S(2)}) async-start(), calls=%async_computation.3 | async-start | bytes 4194304 | tf_op jit(solution)/shard_map/psum | solution.py:11
  171.3 34.3 %copy-start.2 = (f32[128,32,128]{2,0,1:T(8,128)S(1)}, f32[128,32,128]{2,0,1:T(8,128)}, u32[]{:S(2)}) copy-start(f32[128,32,128]{2,0,1:T(8,128)} %all-reduce.9.cloned.1.call-done) | copy-start | bytes 6291460
  228.0 69.1 %copy-start.4 = (f32[16,128,128]{2,1,0:T(8,128)S(1)}, f32[16,128,128]{2,1,0:T(8,128)}, u32[]{:S(2)}) copy-start(f32[16,128,128]{2,1,0:T(8,128)} %all-reduce.11.cloned.1.call-done) | copy-start | bytes 3145732
  228.0 133.3 %all-reduce.15.cloned.1.call-start = ((), (), s32[]{:S(2)}) async-start(), calls=%async_computation.4 | async-start | bytes 2097152 | tf_op jit(solution)/shard_map/psum | solution.py:11
  298.9 2.1 copy-start.1
  301.0 135.8 %all-reduce.17.cloned.1.call-start = ((), (), s32[]{:S(2)}) async-start(), calls=%async_computation.5 | async-start | bytes 4194304 | tf_op jit(solution)/shard_map/psum | solution.py:11
  364.4 72.3 %copy-start.5 = (f32[16,128,128]{2,1,0:T(8,128)S(1)}, f32[16,128,128]{2,1,0:T(8,128)}, u32[]{:S(2)}) copy-start(f32[16,128,128]{2,1,0:T(8,128)} %all-reduce.15.cloned.1.call-done) | copy-start | bytes 3145732
  471.6 23.1 %copy-start = (f32[128,32,128]{2,0,1:T(8,128)S(1)}, f32[128,32,128]{2,0,1:T(8,128)}, u32[]{:S(2)}) copy-start(f32[128,32,128]{2,0,1:T(8,128)} %all-reduce.17.cloned.1.call-done) | copy-start | bytes 6291460
Sparse Core Ops, SparseCore 0:
  40.8 53.5 all-reduce.6
  97.6 69.3 all-reduce.8
  171.4 53.4 all-reduce.10
  228.1 68.8 all-reduce.12
  301.1 53.4 all-reduce.14
  364.6 72.1 all-reduce.16
where the time goes:
time: 547 us; the launch traced here: 543 us
  waiting for transfers between devices  280 us (51%)
  matrix products  107 us (20%)
  local copies, waits for them, and re-layouts  98.3 us (18%)
  other arithmetic  43.4 us (8%)
  between operations  13.6 us (2%)
    psum x6, waiting for transfers between devices, spread(): return lax.psum(kept, axis)  280 us
    dot_general x5, matrix products, update_cols(): jnp.einsum('aij,jcl->aicl', col_panel, rows_sub, precision=lax.Precision....  107 us
    unnamed x14, local copies, waits for them, and re-layouts  55 us
    scatter x1, local copies, waits for them, and re-layouts, update_cols(): return result.at[row_slot].set(replaced)  38.6 us
    concatenate x1, other arithmetic, local(): matrix_local = jnp.concatenate([front, middle, behind], axis=2)  23 us
    scatter x5, other arithmetic, update_cols(): return result.at[row_slot].set(replaced)  11.4 us
  transfers between devices with their start and end apart: 6, of which 5 were waited for; matrix products, arithmetic and copies ran while one was open for 18% of the time, Pallas kernels for 0%

commit v1 on v0

v1 whole, which is shorter than its diff:
```python
import functools

import jax
import jax.numpy as jnp
from jax import lax
from jax.experimental import pallas as pl
from jax.experimental.pallas import tpu as pltpu
from jax.sharding import PartitionSpec as P

PIVOTS = 3
MESH = pl.DeviceIdType.MESH
F32 = jnp.float32
BF16 = jnp.bfloat16


def dot_exact(a, b):
    return jnp.dot(a, b, precision=lax.Precision.HIGHEST, preferred_element_type=F32)


def split(x):
    hi = x.astype(BF16)
    lo = (x - hi.astype(F32)).astype(BF16)
    return hi, lo


def eye_mask(t):
    return lax.broadcasted_iota(jnp.int32, (t, t), 0) == lax.broadcasted_iota(jnp.int32, (t, t), 1)


def newton_inverse(block):
    eye = eye_mask(block.shape[0])
    kept = jnp.where(eye, block, 0.0)
    down = 1.0 / jnp.sum(kept, axis=1, keepdims=True)
    across = 1.0 / jnp.sum(kept, axis=0, keepdims=True)
    return jnp.where(eye, 2.0 * down, 0.0) - down * block * across


def sweep(get, put):
    n = PIVOTS
    a = {(i, j): get(i, j) for i in range(n) for j in range(n)}
    lower, upper = {}, {}
    for p in range(n):
        inverse = newton_inverse(a[p, p])
        rows = {j: inverse if j == p else dot_exact(inverse, a[p, j]) for j in range(n)}
        cols = {i: a[i, p] for i in range(n)}
        for q in range(p + 1):
            lower[p, q] = rows[q]
        for q in range(p):
            upper[q, p] = -cols[q]
        if p + 1 < n:
            for i in range(n):
                if i == p:
                    continue
                for j in range(n):
                    if i < p + 1 and j < p + 1:
                        continue
                    product = dot_exact(cols[i], rows[j])
                    a[i, j] = -product if j == p else a[i, j] - product
            for j in range(n):
                a[p, j] = rows[j]
    for i in range(n):
        for j in range(n):
            total = None
            for s in range(max(i, j), n):
                term = lower[s, j] if s == i else dot_exact(upper[i, s], lower[s, j])
                total = term if total is None else total + term
            put(i, j, total)


def kernel(n_row, n_col, group, blk, mat, out, rows, cols, cells, mix, ccat, rcat,
           load_sem, own_sem, zs_sem, row_recv, col_send, col_recv, cell_send, cell_recv):
    row = lax.axis_index("row")
    col = lax.axis_index("col")
    height, width, t = mat.shape
    n_z = n_row // 2
    n_q = width // group
    z, core = row // 2, lax.rem(row, 2)
    sib = row + 1 - 2 * core
    half = t // 2
    own_half = pl.ds(pl.multiple_of(core * half, half), half)
    other_half = pl.ds(pl.multiple_of((1 - core) * half, half), half)
    out2 = out.reshape(height * width, t)
    rows2 = rows.reshape(PIVOTS * t * width, t)

    loads = [
        pltpu.make_async_copy(
            mat.at[:, pl.ds(q * group, group), :],
            out.at[:, pl.ds(q * group, group), :],
            load_sem.at[q],
        )
        for q in range(n_q)
    ]
    own_rows = pltpu.make_async_copy(mat.at[pl.ds(0, t)], rows.at[jnp.minimum(row, PIVOTS - 1)], own_sem)

    @pl.when(row < PIVOTS)
    def _():
        own_rows.start()

    for load in loads:
        load.start()

    barrier = pltpu.get_barrier_semaphore()
    pl.semaphore_signal(barrier, inc=1, device_id=(sib, col), device_id_type=MESH)

    @pl.when(z > 0)
    def _():
        pl.semaphore_signal(barrier, inc=1, device_id=(row - 2, col), device_id_type=MESH)

    @pl.when(z + 1 < n_z)
    def _():
        pl.semaphore_signal(barrier, inc=1, device_id=(row + 2, col), device_id_type=MESH)

    for d in range(1, n_col):
        pl.semaphore_signal(
            barrier, inc=1, device_id=(row, lax.rem(col + d, n_col)), device_id_type=MESH
        )
    near = jnp.where(z > 0, 1, 0) + jnp.where(z + 1 < n_z, 1, 0)
    pl.semaphore_wait(barrier, n_col + near)

    @pl.when(row < PIVOTS)
    def _():
        own_rows.wait()

    def row_copy(p, q, part, which, kind, target):
        piece = rows.at[p, part, pl.ds(q * group, group), :]
        return pltpu.make_async_remote_copy(
            src_ref=piece,
            dst_ref=piece,
            send_sem=zs_sem.at[p, q, kind],
            recv_sem=row_recv.at[p, q, which],
            device_id=(target, col),
            device_id_type=MESH,
        )

    def row_sends(p, q):
        zp = p // 2
        root = row == p
        return [
            ((z >= zp) & (z + 1 < n_z), row_copy(p, q, own_half, core, 0, row + 2)),
            ((z <= zp) & (z > 0), row_copy(p, q, own_half, core, 1, row - 2)),
            (root, row_copy(p, q, other_half, 1 - core, 2, sib)),
            (root | (z != zp), row_copy(p, q, own_half, core, 3, sib)),
        ]

    def start_sends(p, q):
        for when, copy in row_sends(p, q):
            pl.when(when)(copy.start)

    def root_sends(p, q):
        @pl.when(row == p)
        def _():
            start_sends(p, q)

    def relay(p, q):
        @pl.when(row != p)
        def _():
            row_copy(p, q, own_half, core, 0, sib).wait_recv()
            start_sends(p, q)

    def complete(q):
        for p in range(PIVOTS):
            @pl.when(row != p)
            def _():
                row_copy(p, q, other_half, 1 - core, 0, sib).wait_recv()

    def panel_copy(p, d, part):
        length = height // 2
        piece = cols.at[p, pl.ds(part * length, length), :]
        return pltpu.make_async_remote_copy(
            src_ref=piece,
            dst_ref=piece,
            send_sem=col_send.at[d, part],
            recv_sem=col_recv.at[p, part],
            device_id=(row, lax.rem(col + d, n_col)),
            device_id_type=MESH,
        )

    def cell_copy(p, d):
        return pltpu.make_async_remote_copy(
            src_ref=cells.at[p],
            dst_ref=cells.at[p],
            send_sem=cell_send.at[d],
            recv_sem=cell_recv.at[p],
            device_id=(row, lax.rem(col + d, n_col)),
            device_id_type=MESH,
        )

    def each_root_col(act):
        for p in range(PIVOTS):
            @pl.when(col == p)
            def _():
                act(p)

    def send_panel(part):
        def act(p):
            for d in range(1, n_col):
                panel_copy(p, d, part).start()

        each_root_col(act)

    def wait_panel(part):
        for p in range(PIVOTS):
            @pl.when(col != p)
            def _():
                panel_copy(p, 1, part).wait_recv()

    def take_panel(p):
        @pl.loop(0, height // t)
        def _(b):
            start = pl.multiple_of(b * t, t)
            cols[p, pl.ds(start, t), :] = out2[pl.ds(start * width, t, stride=width), :]

    def send_cells():
        def act(c):
            for p in range(PIVOTS):
                cells[c, pl.ds(p * t, t), :] = rows2[pl.ds(p * t * width, t, stride=width), :]
            for d in range(1, n_col):
                cell_copy(c, d).start()

        each_root_col(act)

    def make_mix():
        for p in range(PIVOTS):
            @pl.when(col != p)
            def _():
                cell_copy(p, 1).wait_recv()

        def put(i, j, value):
            hi, lo = split(value)
            there = pl.ds(j * t, t)
            mix[pl.ds(i * t, t), there] = hi
            mix[pl.ds((PIVOTS + i) * t, t), there] = lo
            mix[pl.ds((2 * PIVOTS + i) * t, t), there] = hi

        sweep(lambda i, j: cells[j, pl.ds(i * t, t), :], put)

    def make_ccat(part):
        eye = jnp.where(eye_mask(t), 1.0, 0.0).astype(F32)
        count = height // t // 2

        @pl.loop(part * count, (part + 1) * count)
        def _(b):
            at = pl.ds(pl.multiple_of(b * t, t), t)
            his, los = [], []
            for p in range(PIVOTS):
                value = cols[p, at, :]
                pivot_rows = (b == 0) & (row < PIVOTS)
                keep = jnp.where(pivot_rows, 0.0, 1.0).astype(F32)
                unit = jnp.where(pivot_rows & (row == p), -1.0, 0.0).astype(F32)
                hi, lo = split(value * keep + eye * unit)
                his.append(hi)
                los.append(lo)
            left = jnp.concatenate(his + his + los, axis=1)
            hi, lo = split(jnp.dot(left, mix[...], preferred_element_type=F32))
            wide = PIVOTS * t
            ccat[at, pl.ds(0, wide)] = hi
            ccat[at, pl.ds(wide, wide)] = hi
            ccat[at, pl.ds(2 * wide, wide)] = lo

    def make_rcat(q):
        eye = jnp.where(eye_mask(t), 1.0, 0.0).astype(F32)
        for j in range(group):
            there = pl.ds(j * t, t)
            for p in range(PIVOTS):
                value = rows2[pl.ds(p * t * width + q * group + j, t, stride=width), :]
                if q == 0 and j == 0:
                    keep = jnp.where(col < PIVOTS, 0.0, 1.0).astype(F32)
                    unit = jnp.where(col == p, 1.0, 0.0).astype(F32)
                    value = value * keep + eye * unit
                hi, lo = split(value)
                rcat[pl.ds(p * t, t), there] = hi
                rcat[pl.ds((PIVOTS + p) * t, t), there] = lo
                rcat[pl.ds((2 * PIVOTS + p) * t, t), there] = hi

    def update(q, first, last):
        n_blk = height // blk

        @pl.loop(n_blk * first // 4, n_blk * last // 4)
        def _(b):
            start = pl.multiple_of(b * blk, blk)
            product = jnp.dot(ccat[pl.ds(start, blk), :], rcat[...], preferred_element_type=F32)
            for j in range(group):
                at = pl.ds(start * width + q * group + j, blk, stride=width)
                out2[at, :] = out2[at, :] - product[:, j * t : (j + 1) * t]

    def clear_base():
        @pl.when(row < PIVOTS)
        def _():
            @pl.loop(0, t)
            def _(i):
                out[i] = jnp.zeros((width, t), F32)

        @pl.when(col < PIVOTS)
        def _():
            @pl.loop(0, height // t)
            def _(b):
                start = pl.multiple_of(b * t, t)
                out2[pl.ds(start * width, t, stride=width), :] = jnp.zeros((t, t), F32)

    order = list(reversed(range(PIVOTS)))
    for p in order:
        root_sends(p, 0)
    loads[0].wait()
    each_root_col(take_panel)
    send_panel(0)
    work = []
    for q in range(n_q):
        for p in order:
            if q > 0:
                root_sends(p, q)
            relay(p, q)
            if work and q > 0:
                work.pop(0)()
        complete(q)
        if q == 0:
            send_cells()
            send_panel(1)

            def base():
                for load in loads[1:]:
                    load.wait()
                clear_base()

            def left():
                wait_panel(0)
                make_ccat(0)

            def rest():
                wait_panel(1)
                make_ccat(1)

            work += [base, lambda: None, lambda: None, make_mix, left, rest]
        parts = 4 if q == n_q - 1 else 2
        if q == 0:
            parts = 2
        for k in range(parts):
            def some(q=q, k=k, parts=parts):
                if k == 0:
                    make_rcat(q)
                update(q, 4 * k // parts, 4 * (k + 1) // parts)

            work.append(some)
    for act in work:
        act()

    for q in range(n_q):
        for p in range(PIVOTS):
            for when, copy in row_sends(p, q):
                pl.when(when)(copy.wait_send)

    def drain(p):
        for d in range(1, n_col):
            panel_copy(p, d, 0).wait_send()
            panel_copy(p, d, 1).wait_send()
            cell_copy(p, d).wait_send()

    each_root_col(drain)


def local(matrix):
    n_row = lax.axis_size("row")
    n_col = lax.axis_size("col")
    row_tiles, _, t, col_tiles, _, _ = matrix.shape
    height = row_tiles * t
    assert n_row % 2 == 0 and PIVOTS <= min(n_row, n_col)
    group = min(8, col_tiles)
    n_q = col_tiles // group
    blk = min(256, height // 4)
    flat = matrix.reshape(height, col_tiles, t)
    wide = PIVOTS * t
    result = pl.pallas_call(
        functools.partial(kernel, n_row, n_col, group, blk),
        out_shape=OUT(flat.shape, F32),
        in_specs=[pl.BlockSpec(memory_space=pl.ANY)],
        out_specs=pl.BlockSpec(memory_space=OUT_SPACE),
        scratch_shapes=[
            pltpu.VMEM((PIVOTS, t, col_tiles, t), F32),
            pltpu.VMEM((PIVOTS, height, t), F32),
            pltpu.VMEM((PIVOTS, wide, t), F32),
            pltpu.VMEM((3 * wide, wide), BF16),
            pltpu.VMEM((height, 3 * wide), BF16),
            pltpu.VMEM((3 * wide, group * t), BF16),
            pltpu.SemaphoreType.DMA((n_q,)),
            pltpu.SemaphoreType.DMA,
            pltpu.SemaphoreType.DMA((PIVOTS, n_q, 4)),
            pltpu.SemaphoreType.DMA((PIVOTS, n_q, 2)),
            pltpu.SemaphoreType.DMA((n_col, 2)),
            pltpu.SemaphoreType.DMA((PIVOTS, 2)),
            pltpu.SemaphoreType.DMA((n_col,)),
            pltpu.SemaphoreType.DMA((PIVOTS,)),
        ],
        compiler_params=pltpu.CompilerParams(
            collective_id=0, has_side_effects=True, vmem_limit_bytes=VMEM_LIMIT
        ),
        cost_estimate=pl.CostEstimate(
            flops=6 * height * wide * col_tiles * t,
            bytes_accessed=8 * height * col_tiles * t,
            transcendentals=0,
        ),
    )(flat)
    return result.reshape(matrix.shape)


OUT = pltpu.VMEM
OUT_SPACE = pltpu.VMEM
VMEM_LIMIT = 26 * 2**20


def solution(mesh):
    in_specs = (P(None, "row", None, None, "col", None),)
    out_specs = P(None, "row", None, None, "col", None)
    return jax.shard_map(local, mesh=mesh, in_specs=in_specs, out_specs=out_specs, check_vma=False)
```

time: 547 us -> 187 us (0.34)
  waiting for transfers between devices: 280 us -> 0 us
  Pallas kernels: 0 us -> 175 us
  matrix products: 107 us -> 0 us
  local copies, waits for them, and re-layouts: 98.3 us -> 11.7 us
  other arithmetic: 43.4 us -> 0 us
  between operations: 13.6 us -> 0.01 us
    psum x6 -> x0, waiting for transfers between devices: 280 us -> none  [spread(): return lax.psum(kept, axis)]
    pallas_call x0 -> x1, Pallas kernels: none -> 175 us  [local(): pl.pallas_call(functools.partial(kernel, n_row, n_col, group, blk), out_s...]
    dot_general x5 -> x0, matrix products: 107 us -> none  [update_cols(): jnp.einsum('aij,jcl->aicl', col_panel, rows_sub, precision=lax.Precision....]
    unnamed x14 -> x1, local copies, waits for them, and re-layouts: 55 us -> 11.7 us
    scatter x1 -> x0, local copies, waits for them, and re-layouts: 38.6 us -> none  [update_cols(): return result.at[row_slot].set(replaced)]
    concatenate x2 -> x0, other arithmetic: 23 us -> none  [the longest x1 23 us: local(): matrix_local = jnp.concatenate([front, middle, behind], axis=2)]
    scatter x5 -> x0, other arithmetic: 11.4 us -> none  [update_cols(): return result.at[row_slot].set(replaced)]
    select_n x6 -> x0, other arithmetic: 9.02 us -> none  [spread(): jnp.where(lax.axis_index(axis) == source, value, 0).astype(value.dtype)]
  transfers between devices with their start and end apart: 6 -> 0, of which waited for: 5 -> 0; matrix products, arithmetic and copies ran while one was open for 18% -> 0% of each run, Pallas kernels for 0% -> 0%
where the time goes in v1:
time: 187 us
  Pallas kernels  175 us (94%)
  local copies, waits for them, and re-layouts  11.7 us (6%)
    pallas_call x1, Pallas kernels, local(): pl.pallas_call(functools.partial(kernel, n_row, n_col, group, blk), out_s...  175 us
    unnamed x1, local copies, waits for them, and re-layouts  11.7 us

profile of v1, /device:TPU:24, one launch (start us, length us, event | category | flops | bytes accessed | tf_op | source)
XLA Modules:
  0.0 186.8 jit_solution(18054416401015229162)
XLA Ops:
  0.0 175.1 %shard_map.17 = f32[2048,32,128]{2,1,0:T(8,128)S(1)} custom-call(f32[2048,32,128]{2,1,0:T(8,128)} %bitcast.5), custom_call_target="tpu_custom_call" | custom-call | flops 19327352832 | bytes 67108864 | tf_op jit(solution)/shard_map/pallas_call | solution.py:371
  175.1 11.7 %copy.4 = f32[16,1,128,32,1,128]{5,4,3,2,1,0:T(1,128)} copy(f32[16,1,128,32,1,128]{5,4,3,2,1,0:T(1,128)S(1)} %bitcast.4) | data formatting | bytes 67108864

commit v2 on v1

--- a/solution.py
+++ b/solution.py
@@ -25,6 +25,20 @@
 
 def eye_mask(t):
     return lax.broadcasted_iota(jnp.int32, (t, t), 0) == lax.broadcasted_iota(jnp.int32, (t, t), 1)
+
+
+def turn(tiles):
+    tiles = list(tiles)
+    place = lax.broadcasted_iota(jnp.int32, tiles[0].shape, 1)
+    for k in (1, 2, 4):
+        low = (place // k) % 2 == 0
+        for j in range(8):
+            if (j // k) % 2:
+                continue
+            a, b = tiles[j], tiles[j + k]
+            tiles[j] = jnp.where(low, a, pltpu.roll(b, k, 1))
+            tiles[j + k] = jnp.where(low, pltpu.roll(a, 8 - k, 1), b)
+    return tiles
 
 
 def newton_inverse(block):
@@ -80,6 +94,8 @@
     own_half = pl.ds(pl.multiple_of(core * half, half), half)
     other_half = pl.ds(pl.multiple_of((1 - core) * half, half), half)
     out2 = out.reshape(height * width, t)
+    out8 = out.reshape(height // 8, 8, width, t)
+    step = 32
     rows2 = rows.reshape(PIVOTS * t * width, t)
 
     loads = [
@@ -279,9 +295,13 @@
         def _(b):
             start = pl.multiple_of(b * blk, blk)
             product = jnp.dot(ccat[pl.ds(start, blk), :], rcat[...], preferred_element_type=F32)
-            for j in range(group):
-                at = pl.ds(start * width + q * group + j, blk, stride=width)
-                out2[at, :] = out2[at, :] - product[:, j * t : (j + 1) * t]
+            for k in range(blk // step):
+                part = product[k * step : (k + 1) * step]
+                tiles = [part[:, j * t : (j + 1) * t].reshape(step // 8, 8, t) for j in range(group)]
+                above = pl.multiple_of(start // 8 + k * (step // 8), step // 8)
+                for i, tile in enumerate(turn(tiles)):
+                    at = (pl.ds(above, step // 8), i, pl.ds(q * group, group), slice(None))
+                    out8[at] = out8[at] - tile
 
     def clear_base():
         @pl.when(row < PIVOTS)
@@ -298,23 +318,39 @@
                 out2[pl.ds(start * width, t, stride=width), :] = jnp.zeros((t, t), F32)
 
     order = list(reversed(range(PIVOTS)))
-    for p in order:
-        root_sends(p, 0)
+    for q in range(n_q):
+        for p in order:
+            if p < 2 or q < 2:
+                root_sends(p, q)
     loads[0].wait()
     each_root_col(take_panel)
     send_panel(0)
     work = []
     for q in range(n_q):
         for p in order:
-            if q > 0:
-                root_sends(p, q)
-            relay(p, q)
+            if q == 0 or p >= 2:
+                relay(p, q)
+            else:
+                @pl.when(z != 0)
+                def _():
+                    relay(p, q)
             if work and q > 0:
                 work.pop(0)()
         complete(q)
+        if q + 2 < n_q:
+            for p in order:
+                if p >= 2:
+                    root_sends(p, q + 2)
         if q == 0:
             send_cells()
             send_panel(1)
+
+            @pl.when(z == 0)
+            def _():
+                for later in range(1, n_q):
+                    for p in order:
+                        if p < 2:
+                            relay(p, later)
 
             def base():
                 for load in loads[1:]:
@@ -363,7 +399,8 @@
     row_tiles, _, t, col_tiles, _, _ = matrix.shape
     height = row_tiles * t
     assert n_row % 2 == 0 and PIVOTS <= min(n_row, n_col)
-    group = min(8, col_tiles)
+    group = 8
+    assert col_tiles % group == 0 and t % 32 == 0
     n_q = col_tiles // group
     blk = min(256, height // 4)
     flat = matrix.reshape(height, col_tiles, t)

time: 187 us -> 152 us (0.81)
  Pallas kernels: 175 us -> 138 us
    pallas_call x1, Pallas kernels: 175 us -> 138 us  [local(): pl.pallas_call(functools.partial(kernel, n_row, n_col, group, blk), out_s...]
where the time goes in v2:
time: 152 us; the launch traced here: 150 us
  Pallas kernels  138 us (91%)
  local copies, waits for them, and re-layouts  11.7 us (8%)
    pallas_call x1, Pallas kernels, local(): pl.pallas_call(functools.partial(kernel, n_row, n_col, group, blk), out_s...  138 us
    unnamed x1, local copies, waits for them, and re-layouts  11.7 us

profile of v2, /device:TPU:24, one launch (start us, length us, event | category | flops | bytes accessed | tf_op | source)
XLA Modules:
  0.0 150.2 jit_solution(15283183787097172760)
XLA Ops:
  0.0 138.5 %shard_map.17 = f32[2048,32,128]{2,1,0:T(8,128)S(1)} custom-call(f32[2048,32,128]{2,1,0:T(8,128)} %bitcast.5), custom_call_target="tpu_custom_call" | custom-call | flops 19327352832 | bytes 67108864 | tf_op jit(solution)/shard_map/pallas_call | solution.py:408
  138.5 11.7 %copy.4 = f32[16,1,128,32,1,128]{5,4,3,2,1,0:T(1,128)} copy(f32[16,1,128,32,1,128]{5,4,3,2,1,0:T(1,128)S(1)} %bitcast.4) | data formatting | bytes 67108864

commit v3 on v2

--- a/solution.py
+++ b/solution.py
@@ -325,7 +325,7 @@
     loads[0].wait()
     each_root_col(take_panel)
     send_panel(0)
-    work = []
+    ready, work = [], []
     for q in range(n_q):
         for p in order:
             if q == 0 or p >= 2:
@@ -334,9 +334,11 @@
                 @pl.when(z != 0)
                 def _():
                     relay(p, q)
-            if work and q > 0:
-                work.pop(0)()
         complete(q)
+        if q == n_q - 2:
+            for act in ready:
+                act()
+            ready = []
         if q + 2 < n_q:
             for p in order:
                 if p >= 2:
@@ -365,18 +367,14 @@
                 wait_panel(1)
                 make_ccat(1)
 
-            work += [base, lambda: None, lambda: None, make_mix, left, rest]
-        parts = 4 if q == n_q - 1 else 2
-        if q == 0:
-            parts = 2
-        for k in range(parts):
-            def some(q=q, k=k, parts=parts):
-                if k == 0:
-                    make_rcat(q)
-                update(q, 4 * k // parts, 4 * (k + 1) // parts)
-
-            work.append(some)
-    for act in work:
+            ready = [base, make_mix, left, rest]
+
+        def some(q=q):
+            make_rcat(q)
+            update(q, 0, 4)
+
+        work.append(some)
+    for act in ready + work:
         act()
 
     for q in range(n_q):

time: 152 us -> 167 us (1.099)
  Pallas kernels: 138 us -> 154 us
    pallas_call x1, Pallas kernels: 138 us -> 154 us  [local(): pl.pallas_call(functools.partial(kernel, n_row, n_col, group, blk), out_s...]
where the time goes in v3:
time: 167 us; the launch traced here: 166 us
  Pallas kernels  154 us (92%)
  local copies, waits for them, and re-layouts  11.7 us (7%)
    pallas_call x1, Pallas kernels, local(): pl.pallas_call(functools.partial(kernel, n_row, n_col, group, blk), out_s...  154 us
    unnamed x1, local copies, waits for them, and re-layouts  11.7 us

profile of v3, /device:TPU:24, one launch (start us, length us, event | category | flops | bytes accessed | tf_op | source)
XLA Modules:
  0.0 165.8 jit_solution(888453552229456886)
XLA Ops:
  0.0 154.1 %shard_map.17 = f32[2048,32,128]{2,1,0:T(8,128)S(1)} custom-call(f32[2048,32,128]{2,1,0:T(8,128)} %bitcast.5), custom_call_target="tpu_custom_call" | custom-call | flops 19327352832 | bytes 67108864 | tf_op jit(solution)/shard_map/pallas_call | solution.py:406
  154.1 11.7 %copy.4 = f32[16,1,128,32,1,128]{5,4,3,2,1,0:T(1,128)} copy(f32[16,1,128,32,1,128]{5,4,3,2,1,0:T(1,128)S(1)} %bitcast.4) | data formatting | bytes 67108864
